TPU v7x, 32 devices: a whole 2x2x4 slice. The times are simulated.
32 devices in a mesh: seg: 8 (over z, core), section: 4 (over y, x).
Axes of the slice: x: 2, y: 2, z: 4, core: 2. Of those that a mesh axis runs over, the one named last changes fastest.
Arguments:
- leaving: bfloat16 [8, 4, 272, 4096], P('seg', 'section'), may hold values from -6 to 6
- w_query: bfloat16 [4, 4096, 2048], P('section'), may hold values from -0.09375 to 0.09375
- w_key: bfloat16 [4, 4096, 2048], P('section', None, 'seg'), may hold values from -0.09375 to 0.09375
- w_value: bfloat16 [4, 4096, 4096], P('section', None, 'seg'), may hold values from -0.09375 to 0.09375
- w_gate: bfloat16 [4, 4096], P('section'), may hold values from -0.09375 to 0.09375
- norm_gain: bfloat16 [4, 4096], P('section'), may hold values from 0.5 to 1.5
- memory_matrix: bfloat16 [4, 4096, 2048], P('section', 'seg'), may hold values from -24 to 24
- key_totals: float32 [4, 2048], P('section'), may hold values from 0.02 to 0.5
- doc_starts: int32 [4, 8], P('section'), may hold values 0 or 1
Outputs:
- updated: bfloat16 [8, 4, 272, 4096], P('seg', 'section')
- matrix_next: bfloat16 [4, 4096, 2048], P('section', 'seg')
- totals_next: float32 [4, 2048], P('section')
All inputs are finite; a program needn't handle non-finite values. No bound on the sum of `doc_starts` on one device may be relied on, other than what follows from the above.
Results may differ from a plain program's by a relative error of at most 0.01.
Values may be sent and summed in bfloat16 or wider, within the bound.
A program may use at most 128 MiB of HBM per device.

v0:
```python
import jax
import jax.numpy as jnp
from jax import lax
from jax.sharding import PartitionSpec as P

MEM = 16


highest = lax.Precision.HIGHEST
epsilon = 1e-05


def shifted(shard, axis, by):
    size = lax.axis_size(axis)
    return lax.ppermute(shard, axis, [(i, (i + by) % size) for i in range(size)])


def feature_map(projected):
    return jax.nn.elu(projected) + 1.0


def contract_last(left_rows, right_rows):
    return lax.dot_general(
        left_rows, right_rows, (((1,), (1,)), ((), ())), preferred_element_type=jnp.float32
    )


def contract_first(left_rows, right_rows):
    return lax.dot_general(
        left_rows,
        right_rows,
        (((0,), (0,)), ((), ())),
        precision=highest,
        preferred_element_type=jnp.float32,
    )


def visibility(starts_row):
    seg_total = starts_row.shape[0]
    positions = jnp.arange(seg_total, dtype=jnp.int32)
    last_start = lax.cummax(jnp.where(starts_row == 1, positions, jnp.int32(-1)), axis=0)
    fresh_flag = (last_start < 0).astype(jnp.float32)
    seen_pairs = (
        (positions[:, None] >= last_start[None, :]) & (positions[:, None] < positions[None, :])
    ).astype(jnp.float32)
    seen_final = (positions >= last_start[seg_total - 1]).astype(jnp.float32)
    return (fresh_flag, seen_pairs, seen_final)


def local(
    leaving, w_query, w_key, w_value, w_gate, norm_gain, memory_matrix, key_totals, doc_starts
):
    entering = shifted(leaving, "section", 1)[0, 0]
    row_count = entering.shape[0]
    feature_count = entering.shape[1]
    seg_count = lax.axis_size("seg")
    my_index = lax.axis_index("seg")
    wide_rows = entering.astype(jnp.float32)
    inverse_rms = lax.rsqrt(jnp.mean(wide_rows * wide_rows, axis=-1, keepdims=True) + epsilon)
    normed = (wide_rows * inverse_rms * norm_gain[0].astype(jnp.float32)).astype(jnp.bfloat16)
    queries = feature_map(jnp.dot(normed, w_query[0], preferred_element_type=jnp.float32)).astype(
        jnp.bfloat16
    )
    memory = lax.all_gather(normed[:MEM], "seg", axis=0, tiled=True)
    key_part = feature_map(jnp.dot(memory, w_key[0], preferred_element_type=jnp.float32)).astype(
        jnp.bfloat16
    )
    value_part = jnp.dot(memory, w_value[0], preferred_element_type=jnp.float32)
    gate_rates = jax.nn.sigmoid(jnp.dot(memory, w_gate[0], preferred_element_type=jnp.float32))
    key_rows = lax.all_gather(key_part, "seg", axis=1, tiled=True)
    values = lax.all_to_all(
        value_part.reshape(seg_count, MEM, value_part.shape[1]).astype(jnp.bfloat16),
        "seg",
        split_axis=0,
        concat_axis=2,
        tiled=True,
    ).astype(jnp.float32)[0]
    fresh_flag, seen_pairs, seen_final = visibility(doc_starts[0])
    key_wide = key_rows.astype(jnp.float32)
    key_sums = key_wide.reshape(seg_count, MEM, -1).sum(axis=1)
    totals = fresh_flag[:, None] * key_totals[0][None, :] + jnp.dot(
        seen_pairs.T, key_sums, precision=highest
    )
    total_rows = jnp.repeat(totals, MEM, axis=0)
    key_scales = jnp.maximum(jnp.sum(total_rows * key_wide, axis=-1), 1.0)
    key_gram = contract_last(key_rows, key_rows)
    seen_cols = jnp.repeat(jnp.repeat(seen_pairs, MEM, axis=0), MEM, axis=1)
    mixing = seen_cols * key_gram * (gate_rates / key_scales)[None, :]
    my_keys = lax.dynamic_slice_in_dim(key_rows, my_index * MEM, MEM, 0)
    probes = jnp.concatenate([queries, my_keys], axis=0)
    probed_all = contract_last(probes, lax.all_gather(memory_matrix[0], "seg", axis=0, tiled=True))
    base_read = probed_all[:row_count]
    probed_keys = probed_all[row_count:]
    my_fresh = fresh_flag[my_index]
    my_rates = lax.dynamic_slice_in_dim(gate_rates, my_index * MEM, MEM, 0)
    my_scales = lax.dynamic_slice_in_dim(key_scales, my_index * MEM, MEM, 0)
    initial = my_rates[:, None] * (values - my_fresh * probed_keys / my_scales[:, None])
    writes = jnp.zeros((seg_count * MEM, feature_count), jnp.float32)
    all_initial = lax.all_gather(initial.astype(jnp.bfloat16), "seg", axis=0, tiled=True).astype(
        initial.dtype
    )

    def local_step(step_index, current):
        mix_cols = lax.dynamic_slice_in_dim(mixing, step_index * MEM, MEM, 1)
        own_terms = lax.dynamic_slice_in_dim(all_initial, step_index * MEM, MEM, 0)
        candidate = own_terms - contract_first(mix_cols, current)
        return lax.dynamic_update_slice_in_dim(current, candidate, step_index * MEM, 0)

    writes = lax.fori_loop(0, seg_count, local_step, writes)
    column_mask = jnp.repeat(seen_pairs[:, my_index], MEM)
    similarity = contract_last(queries, key_rows) * column_mask[None, :]
    low_rank = jnp.dot(similarity, writes, precision=highest)
    my_totals = lax.dynamic_slice_in_dim(totals, my_index, 1, 0)
    denominator = jnp.maximum(jnp.sum(queries.astype(jnp.float32) * my_totals, axis=-1), 1.0)
    updated = (wide_rows + (my_fresh * base_read + low_rank) / denominator[:, None]).astype(
        jnp.bfloat16
    )
    slab_width = memory_matrix.shape[1]
    write_cols = lax.dynamic_slice_in_dim(writes, my_index * slab_width, slab_width, 1)
    end_rows = jnp.repeat(seen_final, MEM)
    fresh_end = fresh_flag[seg_count - 1]
    matrix_next = (
        fresh_end * memory_matrix[0].astype(jnp.float32)
        + contract_first(write_cols * end_rows[:, None], key_wide)
    ).astype(jnp.bfloat16)
    totals_next = fresh_end * key_totals[0] + jnp.dot(seen_final, key_sums, precision=highest)
    return (updated[None, None], matrix_next[None], totals_next[None])


def solution(mesh):
    return jax.shard_map(
        local,
        mesh=mesh,
        in_specs=(
            P("seg", "section", None, None),
            P("section", None, None),
            P("section", None, "seg"),
            P("section", None, "seg"),
            P("section", None),
            P("section", None),
            P("section", "seg", None),
            P("section", None),
            P("section", None),
        ),
        out_specs=(P("seg", "section", None, None), P("section", "seg", None), P("section", None)),
        check_vma=False,
    )
```

profile of v0, /device:TPU:0, one launch (start us, length us, event | category | flops | bytes accessed | tf_op | source)
XLA Modules:
  0.0 316.1 jit_solution(3643618088778170623)
XLA Ops:
  7.2 0.0 copy-start
  7.2 0.0 all-gather.5.cloned.1.call-start
  7.2 3.0 collective-permute-start
  10.2 0.7 mul.181
  11.0 48.9 %collective-permute-done = bf16[1,1,272,4096]{3,2,1,0:T(8,128)(2,1)S(1)} collective-permute-done((bf16[1,1,272,4096]{3,2,1,0:T(8,128)(2,1)}, bf16[1,1,272,4096]{3,2,1,0:T(8,128)(2,1)S(1)}, u32[]{:S(2)}, u32[]{:S(2)}) %collective-permute-start) | collective-permute-done | bytes 2228256 | tf_op jit(solution)/shard_map/ppermute | solution.py:15
  59.8 0.5 multiply_reduce_fusion
  60.4 0.8 copy-done.5
  61.2 0.5 convert_bitcast_fusion
  61.7 0.0 copy-start.11
  61.7 0.8 fusion.52
  62.5 0.0 all-gather.5.cloned.1.call-update
  62.5 0.0 all-gather.9.cloned.1.call-start
  62.5 0.7 all-gather.9.cloned.1.call-update
  63.3 0.2 reduce-window.4
  63.5 0.6 fusion.79
  64.1 21.2 %all-gather.5.cloned.1.call-done = bf16[128,4096]{1,0:T(8,128)(2,1)} async-done(((bf16[16,4096]{1,0:T(8,128)(2,1)}), bf16[128,4096]{1,0:T(8,128)(2,1)}) %all-gather.5.cloned.1.call-update) | async-done | bytes 1048592 | tf_op jit(solution)/shard_map/all_gather | solution.py:64
  85.3 1.8 fusion.62
  87.1 15.6 %all_gather.13 = bf16[128,2048]{1,0:T(8,128)(2,1)S(1)} all-gather(bf16[128,256]{1,0:T(8,128)(2,1)S(1)} %fusion.62), channel_id=1, replica_groups=mesh['seg'=8,'section'=4] {'seg'}, dimensions={1}, use_global_device_ids=true | all-gather | bytes 589824 | tf_op jit(solution)/shard_map/all_gather | solution.py:70
  102.7 0.2 bitcast_reduce_fusion
  102.9 0.2 convolution_add_fusion.1
  103.1 0.2 fusion.47
  103.3 3.6 %fusion.40 = bf16[8,16,512]{2,1,0:T(8,128)(2,1)} fusion(bf16[8,16,4096]{2,1,0:T(8,128)(2,1)S(1)} %bitcast.125, bf16[1,4096,512]{2,1,0:T(8,128)(2,1)} %param.14), kind=kOutput, calls=%fused_computation.39 | convolution fusion | flops 536936448 | bytes 5373952 | tf_op jit(solution)/shard_map/dot_general | solution.py:68
  106.9 6.1 %all-to-all-start = ((bf16[8,16,512]{2,1,0:T(8,128)(2,1)}), bf16[8,16,512]{2,1,0:T(8,128)(2,1)S(1)}, u32[]{:S(2)}, u32[]{:S(2)}) async-start(bf16[8,16,512]{2,1,0:T(8,128)(2,1)} %fusion.40), calls=%async_computation | async-start | bytes 262144 | tf_op jit(solution)/shard_map/all_to_all | solution.py:71
  113.0 0.0 all-gather.7.cloned.1.call-start
  113.1 0.0 copy-start.9
  113.1 13.4 %multiply_reduce_fusion.1 = (f32[272]{0:T(512)S(1)}, bf16[272,2048]{1,0:T(8,128)(2,1)}) fusion(f32[2048]{0:T(1024)S(1)} %bitcast.134, bf16[1,4096,2048]{2,1,0:T(8,128)(2,1)} %param.12, bf16[1,1,272,4096]{3,2,1,0:T(8,128)(2,1)} %copy-done.5, f32[4096]{0:T(1024)S(1)} %bitcast.129, f32[272]{0:T(512)S(1)} %add_rsqrt_fusion), kind=kOutput, calls=%fused_computation.30 | convolution fusion | flops 4572315136 | bytes 20146304 | tf_op jit(solution)/shard_map/dot_general | solution.py:61
  126.4 0.4 multiply_divide_fusion
  126.8 0.1 dynamic_slice.38
  126.9 0.1 dynamic_slice.39
  127.0 0.0 all-to-all-done
  127.1 113.7 %all-gather.9.cloned.1.call-done = bf16[1,4096,2048]{2,1,0:T(8,128)(2,1)} async-done(((bf16[1,512,2048]{2,1,0:T(8,128)(2,1)}), bf16[1,4096,2048]{2,1,0:T(8,128)(2,1)}) %all-gather.9.cloned.1.call-update) | async-done | bytes 16777232 | tf_op jit(solution)/shard_map/all_gather | solution.py:91
  240.8 8.9 %fusion.2 = f32[288,4096]{1,0:T(8,128)S(1)} fusion(bf16[1,4096,2048]{2,1,0:T(8,128)(2,1)} %all-gather.9.cloned.1.call-done, bf16[16,2048]{1,0:T(8,128)(2,1)S(1)} %constant_dynamic-slice_fusion.2, bf16[272,2048]{1,0:T(8,128)(2,1)} %get-tuple-element.97), kind=kOutput, calls=%fused_computation.4 | convolution fusion | flops 4834197504 | bytes 22675456 | tf_op jit(solution)/shard_map/dot_general | solution.py:23
  249.7 2.1 copy-done.10
  251.8 1.3 fusion.55
  253.1 0.0 all-gather.7.cloned.1.call-update
  253.2 0.6 slice.20
  253.7 0.1 fusion.69
  253.8 0.1 broadcast_in_dim.52
  253.9 0.1 reshape.95
  254.0 0.1 copy.15
  254.1 0.7 compare_convert_fusion.1
  254.7 0.1 broadcast_in_dim.55
  254.8 0.1 mul.176
  254.9 0.1 broadcast_in_dim.49
  255.0 0.1 mul.155
  255.1 0.8 fusion.71
  255.9 1.3 multiply_add_fusion
  257.1 0.3 fusion.43
  257.5 0.5 convolution_multiply_fusion
  257.9 15.8 %all-gather.7.cloned.1.call-done = bf16[128,4096]{1,0:T(8,128)(2,1)} async-done(((bf16[16,4096]{1,0:T(8,128)(2,1)}), bf16[128,4096]{1,0:T(8,128)(2,1)}) %all-gather.7.cloned.1.call-update) | async-done | bytes 1048592 | tf_op jit(solution)/shard_map/all_gather | solution.py:99
  273.7 2.8 convert_element_type.94
  276.5 0.2 broadcast_in_dim.50
  276.7 17.2 %while.13 = (s32[]{:T(128)}, f32[128,4096]{1,0:T(8,128)S(1)}, f32[128,4096]{1,0:T(8,128)}, f32[128,128]{1,0:T(8,128)S(1)}, s32[]{:T(128)}, /*index=5*/s32[]{:T(128)}, s32[]{:T(128)}, s32[]{:T(128)}) while((s32[]{:T(128)}, f32[128,4096]{1,0:T(8,128)S(1)}, f32[128,4096]{1,0:T(8,128)}, f32[128,128]{1,0:T(8,128)S(1)}, s32[]{:T(128)}, ...), condition=%wide.region_5.6_spmd, body=%wide.region_4.5_spmd.sunk | while | flops 100728840 | bytes 3212423 | solution.py:109
  276.7 2.1 convolution_subtract_fusion.2
  278.8 2.1 convolution_subtract_fusion.2
  281.0 2.1 convolution_subtract_fusion.2
  283.1 2.1 convolution_subtract_fusion.2
  285.3 2.1 convolution_subtract_fusion.2
  287.4 2.1 convolution_subtract_fusion.2
  289.6 2.1 convolution_subtract_fusion.2
  291.7 2.1 convolution_subtract_fusion.2
  293.9 1.4 copy-done.2
  295.2 5.8 %fusion.15 = bf16[1,512,2048]{2,1,0:T(8,128)(2,1)} fusion(bf16[128,2048]{1,0:T(8,128)(2,1)S(1)} %all_gather.13, bf16[1,512,2048]{2,1,0:T(8,128)(2,1)} %param.17, f32[]{:T(128)} %bitcast.22, f32[128,4096]{1,0:T(8,128)S(1)} %get-tuple-element.82, s32[]{:T(128)S(6)} %select_n.60, f32[128]{0:T(128)S(1)} %mul.176), kind=kOutput, calls=%fused_computation.25 | convolution fusion | flops 1614872576 | bytes 4981256 | tf_op jit(solution)/shard_map/dot_general | solution.py:29
  301.0 8.6 %fusion.9 = bf16[1,1,272,4096]{3,2,1,0:T(8,128)(2,1)} fusion(f32[272,128]{1,0:T(8,128)S(1)} %convolution_multiply_fusion, f32[128,4096]{1,0:T(8,128)} %copy-done.2, f32[288,4096]{1,0:T(8,128)} %copy-done.10, bf16[1,1,272,4096]{3,2,1,0:T(8,128)(2,1)S(1)} %copy-done.6, f32[272]{0:T(512)S(1)} %broadcast_maximum_fusion, f32[]{:T(128)} %bitcast.3), kind=kOutput, calls=%fused_computation.16 | convolution fusion | flops 1717960704 | bytes 11150404 | tf_op jit(solution)/shard_map/dot_general | solution.py:112
  (37 shorter events, 0.3 us)
Async XLA Ops:
  7.2 78.1 %copy-start = (bf16[1,4096,256]{2,1,0:T(8,128)(2,1)S(1)}, bf16[1,4096,256]{2,1,0:T(8,128)(2,1)}, u32[]{:S(2)}) copy-start(bf16[1,4096,256]{2,1,0:T(8,128)(2,1)} %param.13) | copy-start | bytes 6291460
  7.2 78.1 %all-gather.5.cloned.1.call-start = ((), (), s32[]{:S(2)}) async-start(), calls=%async_computation.1 | async-start | bytes 1179648 | tf_op jit(solution)/shard_map/all_gather | solution.py:64
  7.2 52.6 %collective-permute-start = (bf16[1,1,272,4096]{3,2,1,0:T(8,128)(2,1)}, bf16[1,1,272,4096]{3,2,1,0:T(8,128)(2,1)S(1)}, u32[]{:S(2)}, u32[]{:S(2)}) collective-permute-start(bf16[1,1,272,4096]{3,2,1,0:T(8,128)(2,1)} %param.11), channel_id=1, source_target_pairs={{0,1},{1,2},{2,3},{3,0},{4,5},{5,6},{6,7},{7,4},{8,9},{9,10},{10,1... | collective-permute-start | bytes 6684680 | tf_op jit(solution)/shard_map/ppermute | solution.py:15
  59.8 1.4 copy-start.5
  61.7 1.6 copy-start.11
  62.5 178.3 %all-gather.9.cloned.1.call-start = ((), (), s32[]{:S(2)}) async-start(), calls=%async_computation.3 | async-start | bytes 18874368 | tf_op jit(solution)/shard_map/all_gather | solution.py:91
  63.3 39.6 %copy-start.8 = (f32[1,2048]{1,0:T(1,128)S(1)}, f32[1,2048]{1,0:T(1,128)}, u32[]{:S(2)}) copy-start(f32[1,2048]{1,0:T(1,128)} %param.18) | copy-start | bytes 24580
  85.3 18.0 %copy-start.3 = (bf16[128,4096]{1,0:T(8,128)(2,1)S(1)}, bf16[128,4096]{1,0:T(8,128)(2,1)}, u32[]{:S(2)}) copy-start(bf16[128,4096]{1,0:T(8,128)(2,1)} %all-gather.5.cloned.1.call-done) | copy-start | bytes 3145732
  106.9 20.1 %all-to-all-start = ((bf16[8,16,512]{2,1,0:T(8,128)(2,1)}), bf16[8,16,512]{2,1,0:T(8,128)(2,1)S(1)}, u32[]{:S(2)}, u32[]{:S(2)}) async-start(bf16[8,16,512]{2,1,0:T(8,128)(2,1)} %fusion.40), calls=%async_computation | async-start | bytes 262144 | tf_op jit(solution)/shard_map/all_to_all | solution.py:71
  113.0 160.7 %all-gather.7.cloned.1.call-start = ((), (), s32[]{:S(2)}) async-start(), calls=%async_computation.2 | async-start | bytes 1179648 | tf_op jit(solution)/shard_map/all_gather | solution.py:99
  113.0 13.4 %copy-start.4 = (bf16[128,4096]{1,0:T(8,128)(2,1)S(1)}, bf16[128,4096]{1,0:T(8,128)(2,1)}, u32[]{:S(2)}) copy-start(bf16[128,4096]{1,0:T(8,128)(2,1)} %all-gather.5.cloned.1.call-done) | copy-start | bytes 3145732
  113.1 13.4 %copy-start.9 = (bf16[1,4096]{1,0:T(2,128)(2,1)S(1)}, bf16[1,4096]{1,0:T(2,128)(2,1)}, u32[]{:S(2)}) copy-start(bf16[1,4096]{1,0:T(2,128)(2,1)} %param.15) | copy-start | bytes 24580
  249.7 2.1 copy-start.10
  249.7 7.7 %copy-start.7 = (bf16[272,2048]{1,0:T(8,128)(2,1)S(1)}, bf16[272,2048]{1,0:T(8,128)(2,1)}, u32[]{:S(2)}) copy-start(bf16[272,2048]{1,0:T(8,128)(2,1)} %get-tuple-element.97) | copy-start | bytes 3342340
  293.9 1.4 copy-start.2
  295.2 5.8 %copy-start.6 = (bf16[1,1,272,4096]{3,2,1,0:T(8,128)(2,1)S(1)}, bf16[1,1,272,4096]{3,2,1,0:T(8,128)(2,1)}, u32[]{:S(2)}) copy-start(bf16[1,1,272,4096]{3,2,1,0:T(8,128)(2,1)} %copy-done.5) | copy-start | bytes 6684676
  301.0 8.6 %copy-start.1 = (bf16[1,4096,256]{2,1,0:T(8,128)(2,1)S(1)}, bf16[1,4096,256]{2,1,0:T(8,128)(2,1)}, u32[]{:S(2)}) copy-start(bf16[1,4096,256]{2,1,0:T(8,128)(2,1)} %param.13) | copy-start | bytes 6291460
Sparse Core Ops, SparseCore 0:
  62.6 22.6 all-gather.4
  86.9 153.8 all-gather.8
  253.3 20.3 all-gather.6
where the time goes:
time: 317 us; the launch traced here: 316 us
  waiting for transfers between devices  200 us (63%)
  matrix products  60.9 us (19%)
  blocking collectives  15.6 us (5%)
  between operations  14 us (4%)
  other arithmetic  9.17 us (3%)
  starting transfers between devices  9.16 us (3%)
  local copies, waits for them, and re-layouts  6.73 us (2%)
    all_gather x1, waiting for transfers between devices, local(): lax.all_gather(memory_matrix[0], 'seg', axis=0, tiled=True)  114 us
    ppermute x1, waiting for transfers between devices, shifted(): lax.ppermute(shard, axis, [(i, (i + by) % size) for i in range(size)])  48.9 us
    dot_general x9, matrix products, contract_first(): lax.dot_general(left_rows, right_rows, (((0,), (0,)), ((), ())), precisio...  22.5 us
    all_gather x1, waiting for transfers between devices, local(): memory = lax.all_gather(normed[:MEM], 'seg', axis=0, tiled=True)  21.2 us
    all_gather x1, waiting for transfers between devices, local(): lax.all_gather(initial.astype(jnp.bfloat16), 'seg', axis=0, tiled=True)  15.8 us
    all_gather x1, blocking collectives, local(): key_rows = lax.all_gather(key_part, 'seg', axis=1, tiled=True)  15.6 us
    dot_general x1, matrix products, local(): jnp.dot(normed, w_query[0], preferred_element_type=jnp.float32)  13.4 us
    dot_general x3, matrix products, contract_last(): lax.dot_general(left_rows, right_rows, (((1,), (1,)), ((), ())), preferre...  9.69 us
  transfers between devices with their start and end apart: 5, of which 4 were waited for; matrix products, arithmetic and copies ran while one was open for 8% of the time, Pallas kernels for 0%

commit v1 on v0

v1 whole, which is shorter than its diff:
```python
import jax
import jax.numpy as jnp
from jax import lax
from jax.sharding import PartitionSpec as P

MEM = 16


highest = lax.Precision.HIGHEST
epsilon = 1e-05


def shifted(shard, axis, by):
    size = lax.axis_size(axis)
    return lax.ppermute(shard, axis, [(i, (i + by) % size) for i in range(size)])


def feature_map(projected):
    return jax.nn.elu(projected) + 1.0


def contract_last(left_rows, right_rows):
    return lax.dot_general(
        left_rows, right_rows, (((1,), (1,)), ((), ())), preferred_element_type=jnp.float32
    )


def contract_first(left_rows, right_rows):
    return lax.dot_general(
        left_rows,
        right_rows,
        (((0,), (0,)), ((), ())),
        precision=highest,
        preferred_element_type=jnp.float32,
    )


def visibility(starts_row):
    seg_total = starts_row.shape[0]
    positions = jnp.arange(seg_total, dtype=jnp.int32)
    last_start = lax.cummax(jnp.where(starts_row == 1, positions, jnp.int32(-1)), axis=0)
    fresh_flag = (last_start < 0).astype(jnp.float32)
    seen_pairs = (
        (positions[:, None] >= last_start[None, :]) & (positions[:, None] < positions[None, :])
    ).astype(jnp.float32)
    seen_final = (positions >= last_start[seg_total - 1]).astype(jnp.float32)
    return (fresh_flag, seen_pairs, seen_final)


def normalized(rows, gain_row):
    wide = rows.astype(jnp.float32)
    inverse_rms = lax.rsqrt(jnp.mean(wide * wide, axis=-1, keepdims=True) + epsilon)
    return (wide * inverse_rms * gain_row.astype(jnp.float32)).astype(jnp.bfloat16)


def solved(mixing, initial):
    size = mixing.shape[0]
    power = -mixing.T
    writes = initial + jnp.dot(power, initial, precision=highest)
    span = 2
    while span < size // MEM:
        power = jnp.dot(power, power, precision=highest)
        writes = writes + jnp.dot(power, writes, precision=highest)
        span *= 2
    return writes


def chain_start(matrix):
    cores = (0, 1)
    inward = [(c, 2 + c) for c in cores] + [(6 + c, 4 + c) for c in cores]
    across = [(2 + c, 4 + c) for c in cores] + [(4 + c, 2 + c) for c in cores]
    from_middle = lax.ppermute(matrix, "seg", across)
    from_outer = lax.ppermute(matrix, "seg", inward)
    from_far = lax.ppermute(from_outer, "seg", across)
    return (matrix, from_outer, from_middle, from_far)


def chain_read(slices, queries):
    cores = (0, 1)
    inward = [(c, 2 + c) for c in cores] + [(6 + c, 4 + c) for c in cores]
    outward = [(b, a) for a, b in inward]
    outward_crossed = [(b, a ^ 1) for a, b in inward]
    swap = [(i, i ^ 1) for i in range(8)]
    rows = queries.shape[0]
    my_index = lax.axis_index("seg")
    core = my_index % 2
    low_half = my_index < 4
    is_outer = (my_index < 2) | (my_index >= 6)
    own, from_outer, from_middle, from_far = slices
    guests = lax.ppermute(queries, "seg", inward)
    chip_rows = jnp.concatenate([queries, lax.ppermute(queries, "seg", swap)], axis=0)
    guest_rows = jnp.concatenate([guests, lax.ppermute(guests, "seg", swap)], axis=0)

    def read(some_rows, piece):
        return contract_last(some_rows, piece).astype(jnp.bfloat16)

    def spread(chip_part, guest_part):
        mine = (chip_part[:rows], lax.ppermute(chip_part[rows:], "seg", swap))
        if guest_part is None:
            return mine, None
        back = (
            lax.ppermute(guest_part[:rows], "seg", outward),
            lax.ppermute(guest_part[rows:], "seg", outward_crossed),
        )
        return mine, back

    own_mine, own_back = spread(read(chip_rows, own), read(guest_rows, own))
    outer_mine, _ = spread(read(chip_rows, from_outer), None)
    both = jnp.concatenate([chip_rows, guest_rows], axis=0)
    middle = read(both, from_middle)
    middle_mine, middle_back = spread(middle[: 2 * rows], middle[2 * rows :])
    far = read(both, from_far)
    far_mine, far_back = spread(far[: 2 * rows], far[2 * rows :])

    def pick(when_outer, when_inner):
        chosen = [jnp.where(is_outer, a, b) for a, b in zip(when_outer, when_inner)]
        first = jnp.where(core == 0, chosen[0], chosen[1])
        second = jnp.where(core == 0, chosen[1], chosen[0])
        return jnp.concatenate([first, second], axis=1)

    ordered = [
        pick(own_mine, outer_mine),
        pick(own_back, own_mine),
        pick(middle_back, middle_mine),
        pick(far_back, far_mine),
    ]
    return jnp.concatenate(
        [jnp.where(low_half, ordered[k], ordered[3 - k]) for k in range(4)], axis=1
    ).astype(jnp.float32)


def local(
    leaving, w_query, w_key, w_value, w_gate, norm_gain, memory_matrix, key_totals, doc_starts
):
    seg_count = lax.axis_size("seg")
    my_index = lax.axis_index("seg")
    memory_rows = shifted(leaving[0, 0, :MEM], "section", 1)
    entering = shifted(leaving, "section", 1)[0, 0]
    matrix = memory_matrix[0]
    chained = seg_count == 8
    if chained:
        slices = chain_start(matrix)
    else:
        whole_matrix = lax.all_gather(matrix, "seg", axis=0, tiled=True)
    memory = lax.all_gather(normalized(memory_rows, norm_gain[0]), "seg", axis=0, tiled=True)
    key_part = feature_map(jnp.dot(memory, w_key[0], preferred_element_type=jnp.float32)).astype(
        jnp.bfloat16
    )
    value_part = jnp.dot(memory, w_value[0], preferred_element_type=jnp.float32)
    gate_rates = jax.nn.sigmoid(jnp.dot(memory, w_gate[0], preferred_element_type=jnp.float32))
    key_rows = lax.all_gather(key_part, "seg", axis=1, tiled=True)
    fresh_flag, seen_pairs, seen_final = visibility(doc_starts[0])
    key_wide = key_rows.astype(jnp.float32)
    key_sums = key_wide.reshape(seg_count, MEM, -1).sum(axis=1)
    totals = fresh_flag[:, None] * key_totals[0][None, :] + jnp.dot(
        seen_pairs.T, key_sums, precision=highest
    )
    total_rows = jnp.repeat(totals, MEM, axis=0)
    key_scales = jnp.maximum(jnp.sum(total_rows * key_wide, axis=-1), 1.0)
    key_gram = contract_last(key_rows, key_rows)
    seen_cols = jnp.repeat(jnp.repeat(seen_pairs, MEM, axis=0), MEM, axis=1)
    mixing = seen_cols * key_gram * (gate_rates / key_scales)[None, :]
    fresh_rows = jnp.repeat(fresh_flag, MEM)
    probed_keys = contract_last(key_rows, matrix)
    initial = gate_rates[:, None] * (
        value_part - (fresh_rows / key_scales)[:, None] * probed_keys
    )
    write_cols = solved(mixing, initial)
    writes = lax.all_gather(write_cols.astype(jnp.bfloat16), "seg", axis=1, tiled=True)
    fresh_end = fresh_flag[seg_count - 1]
    end_rows = jnp.repeat(seen_final, MEM)
    matrix_next = (
        fresh_end * matrix.astype(jnp.float32)
        + contract_first(write_cols * end_rows[:, None], key_wide)
    ).astype(jnp.bfloat16)
    totals_next = fresh_end * key_totals[0] + jnp.dot(seen_final, key_sums, precision=highest)
    normed = normalized(entering, norm_gain[0])
    queries = feature_map(jnp.dot(normed, w_query[0], preferred_element_type=jnp.float32)).astype(
        jnp.bfloat16
    )
    my_fresh = fresh_flag[my_index]
    column_mask = jnp.repeat(seen_pairs[:, my_index], MEM)
    my_totals = lax.dynamic_slice_in_dim(totals, my_index, 1, 0)
    denominator = jnp.maximum(jnp.sum(queries.astype(jnp.float32) * my_totals, axis=-1), 1.0)
    similarity = contract_last(queries, key_rows) * column_mask[None, :]
    low_rank = jnp.dot(
        similarity.astype(jnp.bfloat16), writes, preferred_element_type=jnp.float32
    )
    if chained:
        base_read = chain_read(slices, queries)
    else:
        base_read = contract_last(queries, whole_matrix)
    updated = (
        entering.astype(jnp.float32) + (my_fresh * base_read + low_rank) / denominator[:, None]
    ).astype(jnp.bfloat16)
    return (updated[None, None], matrix_next[None], totals_next[None])


def solution(mesh):
    return jax.shard_map(
        local,
        mesh=mesh,
        in_specs=(
            P("seg", "section", None, None),
            P("section", None, None),
            P("section", None, "seg"),
            P("section", None, "seg"),
            P("section", None),
            P("section", None),
            P("section", "seg", None),
            P("section", None),
            P("section", None),
        ),
        out_specs=(P("seg", "section", None, None), P("section", "seg", None), P("section", None)),
        check_vma=False,
    )
```

time: 317 us -> 226 us (0.71)
  waiting for transfers between devices: 200 us -> 81 us
  blocking collectives: 15.6 us -> 40 us
  starting transfers between devices: 9.16 us -> 24.3 us
  matrix products: 60.9 us -> 52.1 us
    all_gather x3 -> x2, waiting for transfers between devices: 151 us -> 17 us  [the longest x1 17 us: local(): lax.all_gather(normalized(memory_rows, norm_gain[0]), 'seg', axis=0, tile...]
    ppermute x0 -> x16, waiting for transfers between devices: none -> 60.2 us  [the longest x3 23 us: spread(): lax.ppermute(guest_part[:rows], 'seg', outward)]
    ppermute x1 -> x2, waiting for transfers between devices: 48.9 us -> 3.72 us  [shifted(): lax.ppermute(shard, axis, [(i, (i + by) % size) for i in range(size)])]
    all_gather x1, blocking collectives: 15.6 us -> 40 us  [local(): key_rows = lax.all_gather(key_part, 'seg', axis=1, tiled=True)]
    ppermute x0 -> x16, starting transfers between devices: none -> 20.4 us  [the longest x1 4.85 us: chain_start(): from_outer = lax.ppermute(matrix, 'seg', inward)]
    dot_general x9 -> x1, matrix products: 22.5 us -> 5.56 us  [contract_first(): lax.dot_general(left_rows, right_rows, (((0,), (0,)), ((), ())), precisio...]
    dot_general x3 -> x7, matrix products: 9.69 us -> 20.7 us  [contract_last(): lax.dot_general(left_rows, right_rows, (((1,), (1,)), ((), ())), preferre...]
    all_to_all x1 -> x0, starting transfers between devices: 6.05 us -> none  [local(): lax.all_to_all(value_part.reshape(seg_count, MEM, value_part.shape[1]).as...]
  transfers between devices with their start and end apart: 5 -> 20, of which waited for: 4 -> 9; matrix products, arithmetic and copies ran while one was open for 8% -> 25% of each run, Pallas kernels for 0% -> 0%
where the time goes in v1:
time: 226 us; the launch traced here: 225 us
  waiting for transfers between devices  81 us (36%)
  matrix products  52.1 us (23%)
  blocking collectives  40 us (18%)
  starting transfers between devices  24.3 us (11%)
  between operations  14.5 us (6%)
  other arithmetic  8.97 us (4%)
  local copies, waits for them, and re-layouts  4.1 us (2%)
    all_gather x1, blocking collectives, local(): key_rows = lax.all_gather(key_part, 'seg', axis=1, tiled=True)  40 us
    ppermute x3, waiting for transfers between devices, spread(): lax.ppermute(guest_part[:rows], 'seg', outward)  23 us
    ppermute x1, waiting for transfers between devices, chain_read(): guests = lax.ppermute(queries, 'seg', inward)  21.8 us
    dot_general x7, matrix products, contract_last(): lax.dot_general(left_rows, right_rows, (((1,), (1,)), ((), ())), preferre...  20.7 us
    all_gather x1, waiting for transfers between devices, local(): lax.all_gather(normalized(memory_rows, norm_gain[0]), 'seg', axis=0, tile...  17 us
    ppermute x3, waiting for transfers between devices, spread(): lax.ppermute(guest_part[rows:], 'seg', outward_crossed)  15.4 us
    dot_general x1, matrix products, local(): jnp.dot(normed, w_query[0], preferred_element_type=jnp.float32)  13.1 us
    dot_general x1, matrix products, local(): jnp.dot(similarity.astype(jnp.bfloat16), writes, preferred_element_type=j...  6.48 us
  transfers between devices with their start and end apart: 20, of which 9 were waited for; matrix products, arithmetic and copies ran while one was open for 25% of the time, Pallas kernels for 0%

profile of v1, /device:TPU:0, one launch (start us, length us, event | category | flops | bytes accessed | tf_op | source)
XLA Modules:
  0.0 225.0 jit_solution(18136160995717655431)
XLA Ops:
  7.2 1.1 slice_bitcast_fusion
  8.3 3.0 %collective-permute-start.17 = (bf16[16,4096]{1,0:T(8,128)(2,1)S(1)}, bf16[16,4096]{1,0:T(8,128)(2,1)S(1)}, u32[]{:S(2)}, u32[]{:S(2)}) collective-permute-start(bf16[16,4096]{1,0:T(8,128)(2,1)S(1)} %slice_bitcast_fusion), channel_id=1, source_target_pairs={{0,1},{1,2},{2,3},{3,0},{4,5},{5,6},{6,7},{7,4},{8,9},{9,10},{10,1... | collective-permute-start | bytes 393224 | tf_op jit(solution)/shard_map/ppermute | solution.py:15
  11.3 0.7 mul.176
  12.0 3.7 %collective-permute-done.17 = bf16[16,4096]{1,0:T(8,128)(2,1)S(1)} collective-permute-done((bf16[16,4096]{1,0:T(8,128)(2,1)S(1)}, bf16[16,4096]{1,0:T(8,128)(2,1)S(1)}, u32[]{:S(2)}, u32[]{:S(2)}) %collective-permute-start.17) | collective-permute-done | bytes 131104 | tf_op jit(solution)/shard_map/ppermute | solution.py:15
  15.7 0.1 fusion.54
  15.9 0.8 fusion.56
  16.7 0.8 collective-permute-start
  17.6 4.8 %collective-permute-start.2 = (bf16[512,2048]{1,0:T(8,128)(2,1)}, bf16[512,2048]{1,0:T(8,128)(2,1)}, u32[]{:S(2)}, u32[]{:S(2)}) collective-permute-start(bf16[512,2048]{1,0:T(8,128)(2,1)} %bitcast.124), channel_id=1, source_target_pairs={{0,8},{4,12},{24,16},{28,20},{1,9},{5,13},{25,17},{29,21},{2,10},{... | collective-permute-start | bytes 6291464 | tf_op jit(solution)/shard_map/ppermute | solution.py:73
  22.4 2.0 collective-permute-start.13
  24.4 0.7 bitcast_select_fusion
  25.0 0.2 reduce-window.4
  25.2 0.6 slice.80
  26.2 0.1 copy.13
  26.5 0.7 compare_convert_fusion.1
  27.3 0.6 fusion.90
  28.0 17.0 %all-gather.3.cloned.1.call-done = bf16[128,4096]{1,0:T(8,128)(2,1)} async-done(((bf16[16,4096]{1,0:T(8,128)(2,1)}), bf16[128,4096]{1,0:T(8,128)(2,1)}) %all-gather.3.cloned.1.call-update) | async-done | bytes 1048592 | tf_op jit(solution)/shard_map/all_gather | solution.py:145
  45.0 1.8 fusion.64
  46.8 40.0 %all_gather.10 = bf16[128,2048]{1,0:T(8,128)(2,1)S(1)} all-gather(bf16[128,256]{1,0:T(8,128)(2,1)S(1)} %fusion.64), channel_id=1, replica_groups=mesh['seg'=8,'section'=4] {'seg'}, dimensions={1}, use_global_device_ids=true | all-gather | bytes 589824 | tf_op jit(solution)/shard_map/all_gather | solution.py:151
  86.8 0.2 bitcast_reduce_fusion
  87.0 0.2 convolution_add_fusion.1
  87.2 0.2 fusion.53
  87.4 0.4 multiply_divide_fusion
  87.8 0.3 fusion.49
  88.1 0.3 fusion.92
  88.4 0.7 fusion.10
  89.2 0.9 copy-done.2
  90.0 0.9 fusion.46
  90.9 0.4 convolution_add_fusion.4
  91.3 2.1 fusion.7
  93.5 13.1 %multiply_reduce_fusion = (f32[272]{0:T(512)S(1)}, bf16[272,2048]{1,0:T(8,128)(2,1)}) fusion(f32[2048]{0:T(1024)S(1)} %bitcast.133, bf16[1,4096,2048]{2,1,0:T(8,128)(2,1)} %param.10, bf16[1,1,272,4096]{3,2,1,0:T(8,128)(2,1)} %collective-permute-done, f32[4096]{0:T(1024)S(1)} %bitcast.128, f32[272]{0:T(512)S(1)} %add_rsqrt_fusion), kind=kOutput, calls=%fused_computation.31 | convolution fusion | flops 4572315136 | bytes 20146304 | tf_op jit(solution)/shard_map/dot_general | solution.py:178
  106.6 2.3 %collective-permute-start.5 = (bf16[272,2048]{1,0:T(8,128)(2,1)}, bf16[272,2048]{1,0:T(8,128)(2,1)}, u32[]{:S(2)}, u32[]{:S(2)}) collective-permute-start(bf16[272,2048]{1,0:T(8,128)(2,1)} %get-tuple-element.33), channel_id=1, source_target_pairs={{0,8},{4,12},{24,16},{28,20},{1,9},{5,13},{25,17},{29,21},{2,10},{... | collective-permute-start | bytes 3342344 | tf_op jit(solution)/shard_map/ppermute | solution.py:90
  108.9 0.4 convolution_add_fusion.3
  109.3 2.1 collective-permute-start.7
  111.4 0.2 fusion.93
  111.6 0.4 collective-permute-start.1
  112.0 1.0 fusion.91
  113.0 0.8 fusion.74
  113.8 5.6 %fusion.12 = bf16[1,512,2048]{2,1,0:T(8,128)(2,1)} fusion(bf16[128,2048]{1,0:T(8,128)(2,1)S(1)} %all_gather.10, f32[]{:T(128)} %bitcast.19, f32[128,512]{1,0:T(8,128)S(1)} %get-tuple-element.31, f32[128]{0:T(128)S(1)} %mul.171, bf16[1,512,2048]{2,1,0:T(8,128)(2,1)} %param.15), kind=kOutput, calls=%fused_computation.21 | convolution fusion | flops 1614872576 | bytes 4981252 | tf_op jit(solution)/shard_map/dot_general | solution.py:29
  119.4 21.8 %collective-permute-done.5 = bf16[272,2048]{1,0:T(8,128)(2,1)} collective-permute-done((bf16[272,2048]{1,0:T(8,128)(2,1)}, bf16[272,2048]{1,0:T(8,128)(2,1)}, u32[]{:S(2)}, u32[]{:S(2)}) %collective-permute-start.5) | collective-permute-done | bytes 1114144 | tf_op jit(solution)/shard_map/ppermute | solution.py:90
  141.3 1.2 multiply_add_fusion
  142.5 3.8 %fusion.41 = bf16[544,512]{1,0:T(8,128)(2,1)S(1)} fusion(bf16[512,2048]{1,0:T(8,128)(2,1)} %collective-permute-done.2, bf16[272,2048]{1,0:T(8,128)(2,1)} %collective-permute-done.1, bf16[272,2048]{1,0:T(8,128)(2,1)} %get-tuple-element.33), kind=kOutput, calls=%fused_computation.40 | convolution fusion | flops 1145585664 | bytes 4882432 | tf_op jit(solution)/shard_map/dot_general | solution.py:23
  146.3 2.9 %fusion.40 = bf16[544,512]{1,0:T(8,128)(2,1)S(1)} fusion(bf16[272,2048]{1,0:T(8,128)(2,1)} %collective-permute-done.1, bf16[272,2048]{1,0:T(8,128)(2,1)} %get-tuple-element.33, bf16[1,512,2048]{2,1,0:T(8,128)(2,1)S(1)} %copy-done.3), kind=kOutput, calls=%fused_computation.39 | convolution fusion | flops 1145585664 | bytes 4882432 | tf_op jit(solution)/shard_map/dot_general | solution.py:23
  149.3 5.1 %convolution_convert_fusion.1 = bf16[1088,512]{1,0:T(8,128)(2,1)S(1)} fusion(bf16[512,2048]{1,0:T(8,128)(2,1)} %collective-permute-done.7, bf16[272,2048]{1,0:T(8,128)(2,1)S(1)} %collective-permute-done.6, bf16[272,2048]{1,0:T(8,128)(2,1)} %collective-permute-done.5, bf16[272,2048]{1,0:T(8,128)(2,1)} %collective-permute-done.1, ...), kind=kOutput, calls=%fused_computation.20 | convolution fusion | flops 2300084224 | bytes 7667712 | tf_op jit(solution)/shard_map/dot_general | solution.py:23
  154.5 0.6 collective-permute-start.10
  155.1 1.3 collective-permute-start.8
  156.3 1.3 collective-permute-start.9
  157.7 5.1 %convolution_convert_fusion = bf16[1088,512]{1,0:T(8,128)(2,1)S(1)} fusion(bf16[512,2048]{1,0:T(8,128)(2,1)} %collective-permute-done.13, bf16[272,2048]{1,0:T(8,128)(2,1)S(1)} %collective-permute-done.6, bf16[272,2048]{1,0:T(8,128)(2,1)} %collective-permute-done.5, bf16[272,2048]{1,0:T(8,128)(2,1)} %collective-permute-done.1, ...), kind=kOutput, calls=%fused_computation.19 | convolution fusion | flops 2300084224 | bytes 7667712 | tf_op jit(solution)/shard_map/dot_general | solution.py:23
  162.9 1.3 collective-permute-start.14
  164.2 1.3 collective-permute-start.15
  165.5 2.6 %fusion.42 = bf16[544,512]{1,0:T(8,128)(2,1)S(1)} fusion(bf16[272,2048]{1,0:T(8,128)(2,1)S(1)} %collective-permute-done.6, bf16[272,2048]{1,0:T(8,128)(2,1)} %collective-permute-done.5, bf16[1,512,2048]{2,1,0:T(8,128)(2,1)S(1)} %copy-done.3), kind=kOutput, calls=%fused_computation.41 | convolution fusion | flops 1145585664 | bytes 4882432 | tf_op jit(solution)/shard_map/dot_general | solution.py:23
  168.1 0.1 collective-permute-start.16
  168.2 12.2 %collective-permute-done.8 = bf16[272,512]{1,0:T(8,128)(2,1)S(1)} collective-permute-done((bf16[272,512]{1,0:T(8,128)(2,1)S(1)}, bf16[272,512]{1,0:T(8,128)(2,1)S(1)}, u32[]{:S(2)}, u32[]{:S(2)}) %collective-permute-start.8) | collective-permute-done | bytes 278560 | tf_op jit(solution)/shard_map/ppermute | solution.py:102
  180.4 5.6 %collective-permute-done.9 = bf16[272,512]{1,0:T(8,128)(2,1)S(1)} collective-permute-done((bf16[272,512]{1,0:T(8,128)(2,1)S(1)}, bf16[272,512]{1,0:T(8,128)(2,1)S(1)}, u32[]{:S(2)}, u32[]{:S(2)}) %collective-permute-start.9) | collective-permute-done | bytes 278560 | tf_op jit(solution)/shard_map/ppermute | solution.py:103
  185.9 0.2 collective-permute-start.3
  186.2 6.1 %collective-permute-done.14 = bf16[272,512]{1,0:T(8,128)(2,1)S(1)} collective-permute-done((bf16[272,512]{1,0:T(8,128)(2,1)S(1)}, bf16[272,512]{1,0:T(8,128)(2,1)S(1)}, u32[]{:S(2)}, u32[]{:S(2)}) %collective-permute-start.14) | collective-permute-done | bytes 278560 | tf_op jit(solution)/shard_map/ppermute | solution.py:102
  192.3 1.3 collective-permute-start.11
  193.6 4.3 %collective-permute-done.15 = bf16[272,512]{1,0:T(8,128)(2,1)S(1)} collective-permute-done((bf16[272,512]{1,0:T(8,128)(2,1)S(1)}, bf16[272,512]{1,0:T(8,128)(2,1)S(1)}, u32[]{:S(2)}, u32[]{:S(2)}) %collective-permute-start.15) | collective-permute-done | bytes 278560 | tf_op jit(solution)/shard_map/ppermute | solution.py:103
  197.9 1.5 collective-permute-start.12
  199.5 0.1 broadcast_select_fusion.10
  199.6 4.7 %collective-permute-done.11 = bf16[272,512]{1,0:T(8,128)(2,1)S(1)} collective-permute-done((bf16[272,512]{1,0:T(8,128)(2,1)S(1)}, bf16[272,512]{1,0:T(8,128)(2,1)S(1)}, u32[]{:S(2)}, u32[]{:S(2)}) %collective-permute-start.11) | collective-permute-done | bytes 278560 | tf_op jit(solution)/shard_map/ppermute | solution.py:102
  204.2 5.6 %collective-permute-done.12 = bf16[272,512]{1,0:T(8,128)(2,1)S(1)} collective-permute-done((bf16[272,512]{1,0:T(8,128)(2,1)S(1)}, bf16[272,512]{1,0:T(8,128)(2,1)S(1)}, u32[]{:S(2)}, u32[]{:S(2)}) %collective-permute-start.12) | collective-permute-done | bytes 278560 | tf_op jit(solution)/shard_map/ppermute | solution.py:103
  209.8 0.1 broadcast_select_fusion.12
  209.9 1.7 broadcast_select_fusion.2
  211.6 6.5 %fusion.6 = bf16[1,1,272,4096]{3,2,1,0:T(8,128)(2,1)} fusion(bf16[128,4096]{1,0:T(8,128)(2,1)} %all-gather.5.cloned.1.call-done, bf16[1,1,272,4096]{3,2,1,0:T(8,128)(2,1)} %collective-permute-done, bf16[272,1024]{1,0:T(8,128)(2,1)} %get-tuple-element.34, bf16[272,1024]{1,0:T(8,128)(2,1)} %get-tuple-element.14, bf16[272,1024]{1,0:T(8,128)(2,1)S(1)} %get-tuple-element.13, ...), kind=kOutput, calls=%fused_computation.11 | convolution fusion | flops 443486208 | bytes 9373252 | tf_op jit(solution)/shard_map/dot_general | solution.py:186
  (52 shorter events, 1.2 us)
Async XLA Ops:
  7.2 37.8 %copy-start = (bf16[1,4096,256]{2,1,0:T(8,128)(2,1)S(1)}, bf16[1,4096,256]{2,1,0:T(8,128)(2,1)}, u32[]{:S(2)}) copy-start(bf16[1,4096,256]{2,1,0:T(8,128)(2,1)} %param.11) | copy-start | bytes 6291460
  7.2 37.8 %all-gather.3.cloned.1.call-start = ((), (), s32[]{:S(2)}) async-start(), calls=%async_computation | async-start | bytes 1179648 | tf_op jit(solution)/shard_map/all_gather | solution.py:145
  8.3 7.4 %collective-permute-start.17 = (bf16[16,4096]{1,0:T(8,128)(2,1)S(1)}, bf16[16,4096]{1,0:T(8,128)(2,1)S(1)}, u32[]{:S(2)}, u32[]{:S(2)}) collective-permute-start(bf16[16,4096]{1,0:T(8,128)(2,1)S(1)} %slice_bitcast_fusion), channel_id=1, source_target_pairs={{0,1},{1,2},{2,3},{3,0},{4,5},{5,6},{6,7},{7,4},{8,9},{9,10},{10,1... | collective-permute-start | bytes 393224 | tf_op jit(solution)/shard_map/ppermute | solution.py:15
  16.7 195.0 %all-gather.5.cloned.1.call-start = ((), (), s32[]{:S(2)}) async-start(), calls=%async_computation.1 | async-start | bytes 1179648 | tf_op jit(solution)/shard_map/all_gather | solution.py:169
  16.7 74.6 %collective-permute-start = (bf16[1,1,272,4096]{3,2,1,0:T(8,128)(2,1)}, bf16[1,1,272,4096]{3,2,1,0:T(8,128)(2,1)}, u32[]{:S(2)}, u32[]{:S(2)}) collective-permute-start(bf16[1,1,272,4096]{3,2,1,0:T(8,128)(2,1)} %param.9), channel_id=1, source_target_pairs={{0,1},{1,2},{2,3},{3,0},{4,5},{5,6},{6,7},{7,4},{8,9},{9,10},{10,1... | collective-permute-start | bytes 6684680 | tf_op jit(solution)/shard_map/ppermute | solution.py:15
  17.6 91.8 %collective-permute-start.2 = (bf16[512,2048]{1,0:T(8,128)(2,1)}, bf16[512,2048]{1,0:T(8,128)(2,1)}, u32[]{:S(2)}, u32[]{:S(2)}) collective-permute-start(bf16[512,2048]{1,0:T(8,128)(2,1)} %bitcast.124), channel_id=1, source_target_pairs={{0,8},{4,12},{24,16},{28,20},{1,9},{5,13},{25,17},{29,21},{2,10},{... | collective-permute-start | bytes 6291464 | tf_op jit(solution)/shard_map/ppermute | solution.py:73
  22.4 135.2 %collective-permute-start.13 = (bf16[512,2048]{1,0:T(8,128)(2,1)}, bf16[512,2048]{1,0:T(8,128)(2,1)}, u32[]{:S(2)}, u32[]{:S(2)}) collective-permute-start(bf16[512,2048]{1,0:T(8,128)(2,1)} %bitcast.125), channel_id=1, source_target_pairs={{8,16},{12,20},{16,8},{20,12},{9,17},{13,21},{17,9},{21,13},{10,18... | collective-permute-start | bytes 6291464 | tf_op jit(solution)/shard_map/ppermute | solution.py:72
  26.3 60.6 %copy-start.5 = (f32[1,2048]{1,0:T(1,128)S(1)}, f32[1,2048]{1,0:T(1,128)}, u32[]{:S(2)}) copy-start(f32[1,2048]{1,0:T(1,128)} %param.16) | copy-start | bytes 24580
  28.0 59.4 %copy-start.6 = (bf16[1,4096]{1,0:T(2,128)(2,1)S(1)}, bf16[1,4096]{1,0:T(2,128)(2,1)}, u32[]{:S(2)}) copy-start(bf16[1,4096]{1,0:T(2,128)(2,1)} %param.13) | copy-start | bytes 24580
  45.0 42.4 %copy-start.1 = (bf16[128,4096]{1,0:T(8,128)(2,1)S(1)}, bf16[128,4096]{1,0:T(8,128)(2,1)}, u32[]{:S(2)}) copy-start(bf16[128,4096]{1,0:T(8,128)(2,1)} %all-gather.3.cloned.1.call-done) | copy-start | bytes 3145732
  46.8 41.6 %copy-start.4 = (bf16[1,4096,512]{2,1,0:T(8,128)(2,1)S(1)}, bf16[1,4096,512]{2,1,0:T(8,128)(2,1)}, u32[]{:S(2)}) copy-start(bf16[1,4096,512]{2,1,0:T(8,128)(2,1)} %param.12) | copy-start | bytes 12582916
  88.4 1.6 copy-start.2
  106.6 34.6 %collective-permute-start.5 = (bf16[272,2048]{1,0:T(8,128)(2,1)}, bf16[272,2048]{1,0:T(8,128)(2,1)}, u32[]{:S(2)}, u32[]{:S(2)}) collective-permute-start(bf16[272,2048]{1,0:T(8,128)(2,1)} %get-tuple-element.33), channel_id=1, source_target_pairs={{0,8},{4,12},{24,16},{28,20},{1,9},{5,13},{25,17},{29,21},{2,10},{... | collective-permute-start | bytes 3342344 | tf_op jit(solution)/shard_map/ppermute | solution.py:90
  109.3 39.9 %collective-permute-start.7 = (bf16[512,2048]{1,0:T(8,128)(2,1)}, bf16[512,2048]{1,0:T(8,128)(2,1)}, u32[]{:S(2)}, u32[]{:S(2)}) collective-permute-start(bf16[512,2048]{1,0:T(8,128)(2,1)} %collective-permute-done.2), channel_id=1, source_target_pairs={{8,16},{12,20},{16,8},{20,12},{9,17},{13,21},{17,9},{21,13},{10,18... | collective-permute-start | bytes 6291464 | tf_op jit(solution)/shard_map/ppermute | solution.py:74
  111.6 30.9 %collective-permute-start.1 = (bf16[272,2048]{1,0:T(8,128)(2,1)}, bf16[272,2048]{1,0:T(8,128)(2,1)}, u32[]{:S(2)}, u32[]{:S(2)}) collective-permute-start(bf16[272,2048]{1,0:T(8,128)(2,1)} %get-tuple-element.33), channel_id=1, source_target_pairs={{0,4},{4,0},{8,12},{12,8},{16,20},{20,16},{24,28},{28,24},{1,5},{5... | collective-permute-start | bytes 3342344 | tf_op jit(solution)/shard_map/ppermute | solution.py:91
  141.3 8.0 %collective-permute-start.6 = (bf16[272,2048]{1,0:T(8,128)(2,1)}, bf16[272,2048]{1,0:T(8,128)(2,1)S(1)}, u32[]{:S(2)}, u32[]{:S(2)}) collective-permute-start(bf16[272,2048]{1,0:T(8,128)(2,1)} %collective-permute-done.5), channel_id=1, source_target_pairs={{0,4},{4,0},{8,12},{12,8},{16,20},{20,16},{24,28},{28,24},{1,5},{5... | collective-permute-start | bytes 3342344 | tf_op jit(solution)/shard_map/ppermute | solution.py:92
  142.5 3.8 %copy-start.3 = (bf16[1,512,2048]{2,1,0:T(8,128)(2,1)S(1)}, bf16[1,512,2048]{2,1,0:T(8,128)(2,1)}, u32[]{:S(2)}) copy-start(bf16[1,512,2048]{2,1,0:T(8,128)(2,1)} %param.15) | copy-start | bytes 6291460
  154.5 13.6 %collective-permute-start.10 = (bf16[272,512]{1,0:T(8,128)(2,1)S(1)}, bf16[272,512]{1,0:T(8,128)(2,1)S(1)}, u32[]{:S(2)}, u32[]{:S(2)}) collective-permute-start(bf16[272,512]{1,0:T(8,128)(2,1)S(1)} %get-tuple-element.19), channel_id=1, source_target_pairs={{0,4},{4,0},{8,12},{12,8},{16,20},{20,16},{24,28},{28,24},{1,5},{5... | collective-permute-start | bytes 835592 | tf_op jit(solution)/shard_map/ppermute | solution.py:98
  155.1 25.3 %collective-permute-start.8 = (bf16[272,512]{1,0:T(8,128)(2,1)S(1)}, bf16[272,512]{1,0:T(8,128)(2,1)S(1)}, u32[]{:S(2)}, u32[]{:S(2)}) collective-permute-start(bf16[272,512]{1,0:T(8,128)(2,1)S(1)} %get-tuple-element.18), channel_id=1, source_target_pairs={{8,0},{12,4},{16,24},{20,28},{9,1},{13,5},{17,25},{21,29},{10,2},{... | collective-permute-start | bytes 835592 | tf_op jit(solution)/shard_map/ppermute | solution.py:102
  156.3 29.6 %collective-permute-start.9 = (bf16[272,512]{1,0:T(8,128)(2,1)S(1)}, bf16[272,512]{1,0:T(8,128)(2,1)S(1)}, u32[]{:S(2)}, u32[]{:S(2)}) collective-permute-start(bf16[272,512]{1,0:T(8,128)(2,1)S(1)} %get-tuple-element.20), channel_id=1, source_target_pairs={{8,4},{12,0},{16,28},{20,24},{9,5},{13,1},{17,29},{21,25},{10,6},{... | collective-permute-start | bytes 835592 | tf_op jit(solution)/shard_map/ppermute | solution.py:103
  162.9 29.5 %collective-permute-start.14 = (bf16[272,512]{1,0:T(8,128)(2,1)S(1)}, bf16[272,512]{1,0:T(8,128)(2,1)S(1)}, u32[]{:S(2)}, u32[]{:S(2)}) collective-permute-start(bf16[272,512]{1,0:T(8,128)(2,1)S(1)} %get-tuple-element.15), channel_id=1, source_target_pairs={{8,0},{12,4},{16,24},{20,28},{9,1},{13,5},{17,25},{21,29},{10,2},{... | collective-permute-start | bytes 835592 | tf_op jit(solution)/shard_map/ppermute | solution.py:102
  164.2 33.7 %collective-permute-start.15 = (bf16[272,512]{1,0:T(8,128)(2,1)S(1)}, bf16[272,512]{1,0:T(8,128)(2,1)S(1)}, u32[]{:S(2)}, u32[]{:S(2)}) collective-permute-start(bf16[272,512]{1,0:T(8,128)(2,1)S(1)} %get-tuple-element.17), channel_id=1, source_target_pairs={{8,4},{12,0},{16,28},{20,24},{9,5},{13,1},{17,29},{21,25},{10,6},{... | collective-permute-start | bytes 835592 | tf_op jit(solution)/shard_map/ppermute | solution.py:103
  168.1 31.4 %collective-permute-start.16 = (bf16[272,512]{1,0:T(8,128)(2,1)S(1)}, bf16[272,512]{1,0:T(8,128)(2,1)S(1)}, u32[]{:S(2)}, u32[]{:S(2)}) collective-permute-start(bf16[272,512]{1,0:T(8,128)(2,1)S(1)} %get-tuple-element.16), channel_id=1, source_target_pairs={{0,4},{4,0},{8,12},{12,8},{16,20},{20,16},{24,28},{28,24},{1,5},{5... | collective-permute-start | bytes 835592 | tf_op jit(solution)/shard_map/ppermute | solution.py:98
  180.4 19.2 %collective-permute-start.4 = (bf16[272,512]{1,0:T(8,128)(2,1)S(1)}, bf16[272,512]{1,0:T(8,128)(2,1)S(1)}, u32[]{:S(2)}, u32[]{:S(2)}) collective-permute-start(bf16[272,512]{1,0:T(8,128)(2,1)S(1)} %slice.84), channel_id=1, source_target_pairs={{0,4},{4,0},{8,12},{12,8},{16,20},{20,16},{24,28},{28,24},{1,5},{5... | collective-permute-start | bytes 835592 | tf_op jit(solution)/shard_map/ppermute | solution.py:98
  185.9 13.6 %collective-permute-start.3 = (bf16[272,512]{1,0:T(8,128)(2,1)S(1)}, bf16[272,512]{1,0:T(8,128)(2,1)S(1)}, u32[]{:S(2)}, u32[]{:S(2)}) collective-permute-start(bf16[272,512]{1,0:T(8,128)(2,1)S(1)} %slice.83), channel_id=1, source_target_pairs={{0,4},{4,0},{8,12},{12,8},{16,20},{20,16},{24,28},{28,24},{1,5},{5... | collective-permute-start | bytes 835592 | tf_op jit(solution)/shard_map/ppermute | solution.py:98
  192.3 11.9 %collective-permute-start.11 = (bf16[272,512]{1,0:T(8,128)(2,1)S(1)}, bf16[272,512]{1,0:T(8,128)(2,1)S(1)}, u32[]{:S(2)}, u32[]{:S(2)}) collective-permute-start(bf16[272,512]{1,0:T(8,128)(2,1)S(1)} %get-tuple-element.23), channel_id=1, source_target_pairs={{8,0},{12,4},{16,24},{20,28},{9,1},{13,5},{17,25},{21,29},{10,2},{... | collective-permute-start | bytes 835592 | tf_op jit(solution)/shard_map/ppermute | solution.py:102
  197.9 11.9 %collective-permute-start.12 = (bf16[272,512]{1,0:T(8,128)(2,1)S(1)}, bf16[272,512]{1,0:T(8,128)(2,1)S(1)}, u32[]{:S(2)}, u32[]{:S(2)}) collective-permute-start(bf16[272,512]{1,0:T(8,128)(2,1)S(1)} %get-tuple-element.24), channel_id=1, source_target_pairs={{8,4},{12,0},{16,28},{20,24},{9,5},{13,1},{17,29},{21,25},{10,6},{... | collective-permute-start | bytes 835592 | tf_op jit(solution)/shard_map/ppermute | solution.py:103
Sparse Core Ops, SparseCore 0:
  16.8 28.1 all-gather.2
  113.2 27.7 all-gather.4
